TPU v7x, 32 devices: a whole 2x2x4 slice. The times are simulated.
32 devices in a mesh: groups: 2 (over y), depth: 4 (over z), lat: 2 (over x), sub: 2 (over core).
Axes of the slice: x: 2, y: 2, z: 4, core: 2. Of those that a mesh axis runs over, the one named last changes fastest.
Arguments:
- scalar_field: float32 [8, 18, 512, 512], P(('groups', 'depth'), None, 'lat', 'sub'), parts along dimension 0, may hold values from -6 to 6
- bin_index: int32 [8, 16, 512, 512], P(('groups', 'depth'), None, 'lat', 'sub'), parts along dimension 0, may hold values from 0 to 31
- sample_counts: int32 [8, 2, 2], P(('groups', 'depth'), 'lat', 'sub'), parts along dimension 0, may hold values from 1 to 16, as said below
- view_order: int32 [8], P('groups'), parts along dimension 0, may hold values from 0 to 3, each once
- light_dir: float32 [3], replicated, may hold values from -3 to 3
- tf_color: float32 [3, 32], replicated, may hold values from 0.1 to 1
- tf_opacity: float32 [32], replicated, may hold values from 0.005 to 0.08
Outputs:
- final_image: float32 [4, 1024, 512], P(None, ('groups', 'lat'), 'sub'), parts along dimension 1
There are 2 independent parts, one for each index of `groups`. A program takes and returns all parts, laid end to end along the dimension named above; an argument that names none is the same for every part. Nothing has to cross between parts.
Inputs may be any that keep to these rules, and one draw needn't show every extreme that they name: `sample_counts`: one brick and tile of each part has exactly 16. `view_order`: each brick index appears once.
All inputs are finite; a program needn't handle non-finite values.
Results may differ from a plain program's by a relative error of at most 0.0003.
Values sent between devices are 32-bit elements; how exact they have to be, the bound alone decides.
A program may use at most 128 MiB of HBM per device.

v0:
```python
import jax
import jax.numpy as jnp
from jax import lax
from jax.sharding import PartitionSpec as P


def extended(cells, sides, width):
    for axis, dim in sides:
        count = lax.axis_size(axis)
        ends = count - 1
        head = lax.slice_in_dim(cells, 0, width, axis=dim)
        tail = lax.slice_in_dim(cells, cells.shape[dim] - width, cells.shape[dim], axis=dim)
        cells = jnp.concatenate(
            [
                lax.ppermute(tail, axis, [(i, (i + 1) % count) for i in range(ends)]),
                cells,
                lax.ppermute(head, axis, [((i + 1) % count, i) for i in range(ends)]),
            ],
            axis=dim,
        )
    return cells


def shading_terms(padded, depth_step, light_dir):
    below_plane = lax.dynamic_index_in_dim(padded, depth_step, 0, keepdims=False)[1:-1, 1:-1]
    centre_pad = lax.dynamic_index_in_dim(padded, depth_step + 1, 0, keepdims=False)
    above_plane = lax.dynamic_index_in_dim(padded, depth_step + 2, 0, keepdims=False)[1:-1, 1:-1]
    centre = centre_pad[1:-1, 1:-1]
    grad_x = (centre_pad[2:, 1:-1] - centre_pad[:-2, 1:-1]) * 0.5
    grad_y = (centre_pad[1:-1, 2:] - centre_pad[1:-1, :-2]) * 0.5
    grad_z = (above_plane - below_plane) * 0.5
    facing = (grad_x * light_dir[0] + grad_y * light_dir[1] + grad_z * light_dir[2]) / jnp.sqrt(
        grad_x * grad_x + grad_y * grad_y + grad_z * grad_z + 1.0
    )
    shading = 0.25 + 0.5 * jnp.abs(facing)
    return (centre, shading)


def composite(stacked, view_order):
    image_rgb = jnp.zeros((3,) + stacked.shape[2:], jnp.float32)
    image_remain = jnp.ones(stacked.shape[2:], jnp.float32)

    def one_brick(rank_idx, state):
        accum_rgb, remain = state
        partial_value = lax.dynamic_index_in_dim(stacked, view_order[rank_idx], 0, keepdims=False)
        return (accum_rgb + remain * partial_value[:3], remain * partial_value[3])

    image_rgb, image_remain = lax.fori_loop(
        0, stacked.shape[0], one_brick, (image_rgb, image_remain)
    )
    return jnp.concatenate([image_rgb, (1.0 - image_remain)[None]], 0)


def on_device(scalar_field, bin_index, sample_counts, view_order, light_dir, tf_color, tf_opacity):
    padded = extended(scalar_field, (("lat", 2), ("sub", 3)), 1)[0]
    bins_brick = bin_index[0]
    sample_count = sample_counts[0, 0, 0]
    tf_table = jnp.concatenate([tf_color, tf_opacity[None]], 0)
    bin_ids = lax.iota(jnp.int32, tf_table.shape[1])
    rows_here = bins_brick.shape[1]
    cols_here = bins_brick.shape[2]

    def one_plane(depth_step, state):
        accum_rgb, remain = state
        centre, shading = shading_terms(padded, depth_step, light_dir)
        bins_plane = lax.dynamic_index_in_dim(bins_brick, depth_step, 0, keepdims=False)
        choose = bins_plane[None, None] == bin_ids[None, :, None, None]
        looked_up = jnp.sum(jnp.where(choose, tf_table[:, :, None, None], 0.0), axis=1)
        density = looked_up[3] * jax.nn.softplus(centre)
        survive = jnp.exp(-density)
        opacity_now = 1.0 - survive
        accum_rgb = accum_rgb + remain * (looked_up[:3] * (shading * opacity_now)[None])
        return (accum_rgb, remain * survive)

    init = (
        jnp.zeros((3, rows_here, cols_here), jnp.float32),
        jnp.ones((rows_here, cols_here), jnp.float32),
    )
    accum_rgb, remain = lax.fori_loop(0, sample_count, one_plane, init)
    partial_value = jnp.concatenate([accum_rgb, remain[None]], 0)[None]
    all_parts = lax.all_gather(partial_value, "depth", axis=0, tiled=True)
    final_image = composite(all_parts, view_order)
    return final_image


def solution(mesh):
    return jax.shard_map(
        on_device,
        mesh=mesh,
        in_specs=(
            P(("groups", "depth"), None, "lat", "sub"),
            P(("groups", "depth"), None, "lat", "sub"),
            P(("groups", "depth"), "lat", "sub"),
            P("groups"),
            P(),
            P(),
            P(),
        ),
        out_specs=P(None, ("groups", "lat"), "sub"),
        check_vma=False,
    )
```

profile of v0, /device:TPU:0, one launch (start us, length us, event | category | flops | bytes accessed | tf_op | source)
XLA Modules:
  0.0 288.4 jit_solution(1518800508941762854)
XLA Ops:
  7.5 4.8 %collective-permute-start = (f32[1,18,1,256]{3,2,1,0:T(1,128)S(1)}, f32[1,18,1,256]{3,2,1,0:T(1,128)S(1)}, u32[]{:S(2)}, u32[]{:S(2)}) collective-permute-start(f32[1,18,1,256]{3,2,1,0:T(1,128)S(1)} %get-tuple-element.344), channel_id=1, source_target_pairs={{0,2},{1,3},{4,6},{5,7},{8,10},{9,11},{12,14},{13,15},{16,18},{17,... | collective-permute-start | bytes 55304 | tf_op jit(solution)/shard_map/ppermute | solution.py:15
  12.4 1.3 collective-permute-start.1
  13.7 1.4 fusion.12
  15.1 6.0 %copy.17 = f32[1,18,256,256]{2,3,1,0:T(8,128)} copy(f32[1,18,256,256]{3,2,1,0:T(8,128)} %param.11) | data formatting | bytes 9437184 | tf_op args[0]
  21.9 2.2 copy.18
  24.1 1.3 pad_maximum_fusion.4
  25.4 1.5 collective-permute-start.2
  26.9 1.3 collective-permute-start.3
  30.1 7.4 %maximum_bitcast_fusion = f32[18,258,258]{1,2,0:T(8,128)} fusion(f32[1,18,258,1]{2,3,1,0:T(1,128)S(1)} %collective-permute-done.3, f32[1,18,1,256]{2,3,1,0:T(8,128)} %copy.18, f32[1,18,256,256]{2,3,1,0:T(8,128)} %copy.17, f32[1,18,1,256]{2,3,1,0:T(8,128)S(1)} %copy.16, f32[1,18,258,1]{2,3,1,0:T(1,128)S(1)} %collective-permute-done.2), kind=kLoop, calls=%fused_computation.26 | loop fusion | flops 4792608 | bytes 9585216 | tf_op jit(solution)/shard_map/squeeze | solution.py:55
  37.6 8.7 %copy.19 = f32[18,258,258]{2,1,0:T(8,128)} copy(f32[18,258,258]{1,2,0:T(8,128)} %maximum_bitcast_fusion) | data formatting | bytes 9585216
  46.3 90.9 %while.31 = (s32[]{:T(128)}, f32[3,256,256]{2,1,0:T(8,128)S(1)}, f32[256,256]{1,0:T(8,128)S(1)}, s32[]{:T(128)}, s32[16,256,256]{2,1,0:T(8,128)}, /*index=5*/f32...) while((s32[]{:T(128)}, f32[3,256,256]{2,1,0:T(8,128)S(1)}, ...), condition=%wide.region_2.3_spmd.clone, body=%wide.region_0.2_spmd.clone.sunk | while | flops 21299204 | bytes 13919148 | solution.py:79
  47.0 1.3 dynamic-slice_bitcast_fusion.9
  49.3 1.2 iota_compare_fusion.2
  50.6 3.0 %select_reduce_fusion.2 = f32[4,256,256]{2,1,0:T(8,128)S(1)} fusion(f32[4,32]{1,0:T(4,128)S(1)} %get-tuple-element.495, pred[32,256,256]{2,1,0:T(8,128)(4,1)S(1)} %iota_compare_fusion.2), kind=kLoop, calls=%fused_computation.1.clone.1 | loop fusion | flops 16515072 | bytes 3146240 | tf_op jit(solution)/shard_map/while/body/reduce_sum | solution.py:68
  55.2 1.3 dynamic-slice_bitcast_fusion.9
  57.5 1.2 iota_compare_fusion.2
  58.8 3.0 %select_reduce_fusion.2 = f32[4,256,256]{2,1,0:T(8,128)S(1)} fusion(f32[4,32]{1,0:T(4,128)S(1)} %get-tuple-element.495, pred[32,256,256]{2,1,0:T(8,128)(4,1)S(1)} %iota_compare_fusion.2), kind=kLoop, calls=%fused_computation.1.clone.1 | loop fusion | flops 16515072 | bytes 3146240 | tf_op jit(solution)/shard_map/while/body/reduce_sum | solution.py:68
  63.4 1.3 dynamic-slice_bitcast_fusion.9
  65.7 1.2 iota_compare_fusion.2
  67.0 3.0 %select_reduce_fusion.2 = f32[4,256,256]{2,1,0:T(8,128)S(1)} fusion(f32[4,32]{1,0:T(4,128)S(1)} %get-tuple-element.495, pred[32,256,256]{2,1,0:T(8,128)(4,1)S(1)} %iota_compare_fusion.2), kind=kLoop, calls=%fused_computation.1.clone.1 | loop fusion | flops 16515072 | bytes 3146240 | tf_op jit(solution)/shard_map/while/body/reduce_sum | solution.py:68
  71.6 1.3 dynamic-slice_bitcast_fusion.9
  73.9 1.2 iota_compare_fusion.2
  75.2 3.0 %select_reduce_fusion.2 = f32[4,256,256]{2,1,0:T(8,128)S(1)} fusion(f32[4,32]{1,0:T(4,128)S(1)} %get-tuple-element.495, pred[32,256,256]{2,1,0:T(8,128)(4,1)S(1)} %iota_compare_fusion.2), kind=kLoop, calls=%fused_computation.1.clone.1 | loop fusion | flops 16515072 | bytes 3146240 | tf_op jit(solution)/shard_map/while/body/reduce_sum | solution.py:68
  79.8 1.3 dynamic-slice_bitcast_fusion.9
  82.2 1.2 iota_compare_fusion.2
  83.4 3.0 %select_reduce_fusion.2 = f32[4,256,256]{2,1,0:T(8,128)S(1)} fusion(f32[4,32]{1,0:T(4,128)S(1)} %get-tuple-element.495, pred[32,256,256]{2,1,0:T(8,128)(4,1)S(1)} %iota_compare_fusion.2), kind=kLoop, calls=%fused_computation.1.clone.1 | loop fusion | flops 16515072 | bytes 3146240 | tf_op jit(solution)/shard_map/while/body/reduce_sum | solution.py:68
  88.0 1.3 dynamic-slice_bitcast_fusion.9
  90.4 1.2 iota_compare_fusion.2
  91.6 3.0 %select_reduce_fusion.2 = f32[4,256,256]{2,1,0:T(8,128)S(1)} fusion(f32[4,32]{1,0:T(4,128)S(1)} %get-tuple-element.495, pred[32,256,256]{2,1,0:T(8,128)(4,1)S(1)} %iota_compare_fusion.2), kind=kLoop, calls=%fused_computation.1.clone.1 | loop fusion | flops 16515072 | bytes 3146240 | tf_op jit(solution)/shard_map/while/body/reduce_sum | solution.py:68
  96.2 1.3 dynamic-slice_bitcast_fusion.9
  98.6 1.2 iota_compare_fusion.2
  99.8 3.0 %select_reduce_fusion.2 = f32[4,256,256]{2,1,0:T(8,128)S(1)} fusion(f32[4,32]{1,0:T(4,128)S(1)} %get-tuple-element.495, pred[32,256,256]{2,1,0:T(8,128)(4,1)S(1)} %iota_compare_fusion.2), kind=kLoop, calls=%fused_computation.1.clone.1 | loop fusion | flops 16515072 | bytes 3146240 | tf_op jit(solution)/shard_map/while/body/reduce_sum | solution.py:68
  104.4 1.3 dynamic-slice_bitcast_fusion.9
  108.0 3.0 %select_reduce_fusion.2 = f32[4,256,256]{2,1,0:T(8,128)S(1)} fusion(f32[4,32]{1,0:T(4,128)S(1)} %get-tuple-element.495, pred[32,256,256]{2,1,0:T(8,128)(4,1)S(1)} %iota_compare_fusion.2), kind=kLoop, calls=%fused_computation.1.clone.1 | loop fusion | flops 16515072 | bytes 3146240 | tf_op jit(solution)/shard_map/while/body/reduce_sum | solution.py:68
  112.6 1.3 dynamic-slice_bitcast_fusion.9
  116.2 3.0 %select_reduce_fusion.2 = f32[4,256,256]{2,1,0:T(8,128)S(1)} fusion(f32[4,32]{1,0:T(4,128)S(1)} %get-tuple-element.495, pred[32,256,256]{2,1,0:T(8,128)(4,1)S(1)} %iota_compare_fusion.2), kind=kLoop, calls=%fused_computation.1.clone.1 | loop fusion | flops 16515072 | bytes 3146240 | tf_op jit(solution)/shard_map/while/body/reduce_sum | solution.py:68
  120.9 1.3 dynamic-slice_bitcast_fusion.9
  123.2 1.2 iota_compare_fusion.2
  124.4 3.0 %select_reduce_fusion.2 = f32[4,256,256]{2,1,0:T(8,128)S(1)} fusion(f32[4,32]{1,0:T(4,128)S(1)} %get-tuple-element.495, pred[32,256,256]{2,1,0:T(8,128)(4,1)S(1)} %iota_compare_fusion.2), kind=kLoop, calls=%fused_computation.1.clone.1 | loop fusion | flops 16515072 | bytes 3146240 | tf_op jit(solution)/shard_map/while/body/reduce_sum | solution.py:68
  129.1 1.3 dynamic-slice_bitcast_fusion.9
  131.4 1.2 iota_compare_fusion.2
  132.6 3.0 %select_reduce_fusion.2 = f32[4,256,256]{2,1,0:T(8,128)S(1)} fusion(f32[4,32]{1,0:T(4,128)S(1)} %get-tuple-element.495, pred[32,256,256]{2,1,0:T(8,128)(4,1)S(1)} %iota_compare_fusion.2), kind=kLoop, calls=%fused_computation.1.clone.1 | loop fusion | flops 16515072 | bytes 3146240 | tf_op jit(solution)/shard_map/while/body/reduce_sum | solution.py:68
  138.3 122.2 %all-gather.3.cloned.1.call-done = f32[16,256,256]{2,1,0:T(8,128)} async-done(((f32[4,256,256]{2,1,0:T(8,128)}), f32[16,256,256]{2,1,0:T(8,128)}) %all-gather.3.cloned.1.call-update) | async-done | bytes 4194320 | tf_op jit(solution)/shard_map/all_gather | solution.py:81
  260.6 19.9 %while.32 = (s32[]{:T(128)}, f32[3,256,256]{2,1,0:T(8,128)S(1)}, f32[256,256]{1,0:T(8,128)S(1)}, s32[4]{0:T(128)S(1)}, f32[4,4,256,256]{3,2,1,0:T(8,128)}, /*index=5*/s32[]{:T(128)}, s32[]{:T(128)}, s32[]{:T(128)}, s32[]{}) while((s32[]{:T(128)}, f32[3,256,256]{2,1,0:T(8,128)S(1)}, f32[256,256]{1,0:T(8,128)S(1)}, s32[4]{0:T(128)S(1)}, ...), condition=%wide.region_4.5_spmd.clone, body=%wide.region_3.4_spmd.clone.sunk | while | flops 720903 | bytes 3670190 | solution.py:48
  264.1 1.4 fusion.20
  269.1 1.4 fusion.20
  274.1 1.4 fusion.20
  279.1 1.4 fusion.20
  (76 shorter events, 34.1 us)
Async XLA Ops:
  6.5 254.0 %all-gather.3.cloned.1.call-start = ((), (), s32[]{:S(2)}) async-start(), calls=%async_computation | async-start | bytes 5242880 | tf_op jit(solution)/shard_map/all_gather | solution.py:81
  7.5 13.6 %collective-permute-start = (f32[1,18,1,256]{3,2,1,0:T(1,128)S(1)}, f32[1,18,1,256]{3,2,1,0:T(1,128)S(1)}, u32[]{:S(2)}, u32[]{:S(2)}) collective-permute-start(f32[1,18,1,256]{3,2,1,0:T(1,128)S(1)} %get-tuple-element.344), channel_id=1, source_target_pairs={{0,2},{1,3},{4,6},{5,7},{8,10},{9,11},{12,14},{13,15},{16,18},{17,... | collective-permute-start | bytes 55304 | tf_op jit(solution)/shard_map/ppermute | solution.py:15
  12.4 9.5 %collective-permute-start.1 = (f32[1,18,1,256]{3,2,1,0:T(1,128)S(1)}, f32[1,18,1,256]{3,2,1,0:T(1,128)S(1)}, u32[]{:S(2)}, u32[]{:S(2)}) collective-permute-start(f32[1,18,1,256]{3,2,1,0:T(1,128)S(1)} %get-tuple-element.345), channel_id=1, source_target_pairs={{2,0},{3,1},{6,4},{7,5},{10,8},{11,9},{14,12},{15,13},{18,16},{19,... | collective-permute-start | bytes 55304 | tf_op jit(solution)/shard_map/ppermute | solution.py:17
  24.1 4.1 %copy-start = (f32[3,32]{1,0:T(4,128)S(1)}, f32[3,32]{1,0:T(4,128)}, u32[]{:S(2)}) copy-start(f32[3,32]{1,0:T(4,128)} %param.16) | copy-start | bytes 1156
  24.1 4.1 %copy-start.1 = (f32[32]{0:T(128)S(1)}, f32[32]{0:T(128)}, u32[]{:S(2)}) copy-start(f32[32]{0:T(128)} %param.17) | copy-start | bytes 388
  25.4 4.7 %collective-permute-start.2 = (f32[1,18,258,1]{2,3,1,0:T(1,128)S(1)}, f32[1,18,258,1]{2,3,1,0:T(1,128)S(1)}, u32[]{:S(2)}, u32[]{:S(2)}) collective-permute-start(f32[1,18,258,1]{2,3,1,0:T(1,128)S(1)} %get-tuple-element.342), channel_id=1, source_target_pairs={{0,1},{2,3},{4,5},{6,7},{8,9},{10,11},{12,13},{14,15},{16,17},{18,... | collective-permute-start | bytes 55736 | tf_op jit(solution)/shard_map/ppermute | solution.py:15
  26.9 3.3 %collective-permute-start.3 = (f32[1,18,258,1]{2,3,1,0:T(1,128)S(1)}, f32[1,18,258,1]{2,3,1,0:T(1,128)S(1)}, u32[]{:S(2)}, u32[]{:S(2)}) collective-permute-start(f32[1,18,258,1]{2,3,1,0:T(1,128)S(1)} %get-tuple-element.343), channel_id=1, source_target_pairs={{1,0},{3,2},{5,4},{7,6},{9,8},{11,10},{13,12},{15,14},{17,16},{19,... | collective-permute-start | bytes 55736 | tf_op jit(solution)/shard_map/ppermute | solution.py:17
  46.3 214.2 %copy-start.2 = (s32[4]{0:T(128)S(1)}, s32[4]{0:T(128)}, u32[]{:S(2)}) copy-start(s32[4]{0:T(128)} %param.14) | copy-start | bytes 52
Sparse Core Ops, SparseCore 0:
  138.4 122.0 all-gather.2
where the time goes:
time: 291 us; the launch traced here: 288 us
  waiting for transfers between devices  122 us (42%)
  other arithmetic  77.3 us (27%)
  local copies, waits for them, and re-layouts  48 us (16%)
  loops' own time  16.4 us (6%)
  between operations  15.5 us (5%)
  starting transfers between devices  8.89 us (3%)
    all_gather x1, waiting for transfers between devices, on_device(): all_parts = lax.all_gather(partial_value, 'depth', axis=0, tiled=True)  122 us
    reduce_sum x11, other arithmetic, one_plane(): jnp.sum(jnp.where(choose, tf_table[:, :, None, None], 0.0), axis=1)  33.1 us
    unnamed x8, local copies, waits for them, and re-layouts  14.7 us
    squeeze x11, local copies, waits for them, and re-layouts, shading_terms(): lax.dynamic_index_in_dim(padded, depth_step + 1, 0, keepdims=False)  14.6 us
    eq x11, other arithmetic, one_plane(): choose = bins_plane[None, None] == bin_ids[None, :, None, None]  13.3 us
    eq x11, local copies, waits for them, and re-layouts, one_plane(): choose = bins_plane[None, None] == bin_ids[None, :, None, None]  10.7 us
    another operation x1, loops' own time, on_device(): accum_rgb, remain = lax.fori_loop(0, sample_count, one_plane, init)  8.56 us
    another operation x1, loops' own time, composite(): lax.fori_loop(0, stacked.shape[0], one_brick, (image_rgb, image_remain))  7.87 us
  transfers between devices with their start and end apart: 5, of which 1 were waited for; matrix products, arithmetic and copies ran while one was open for 3% of the time, Pallas kernels for 0%

commit v1 on v0

v1 whole, which is shorter than its diff:
```python
import functools
import math

import jax
import jax.numpy as jnp
from jax import lax
from jax.experimental import pallas as pl
from jax.experimental.pallas import tpu as pltpu
from jax.sharding import PartitionSpec as P

MESH = pl.DeviceIdType.MESH
LANES = 128
STRIPS = 8
LAG_SUM = 1
LAG_DONE = 2


def composite(stacked, view_order):
    image_rgb = jnp.zeros((3,) + stacked.shape[2:], jnp.float32)
    image_remain = jnp.ones(stacked.shape[2:], jnp.float32)

    def one_brick(rank_idx, state):
        accum_rgb, remain = state
        partial_value = lax.dynamic_index_in_dim(stacked, view_order[rank_idx], 0, keepdims=False)
        return (accum_rgb + remain * partial_value[:3], remain * partial_value[3])

    image_rgb, image_remain = lax.fori_loop(
        0, stacked.shape[0], one_brick, (image_rgb, image_remain)
    )
    return jnp.concatenate([image_rgb, (1.0 - image_remain)[None]], 0)


def lookup(table, bins):
    return jnp.take_along_axis(table, bins, axis=1, mode="promise_in_bounds")


def kernel(
    n_depth, n_lat, exchange,
    field, bins, counts, order, light, color, opacity, out,
    fv, bv, col_send, col_recv, row_send, row_recv, table,
    part, ends, far_remain, mine, theirs, fin,
    load_sem, col_sem, row_sem, barrier_pad,
    part_sems, part_recv, own_sems, own_recv, far_sems, far_recv,
    sum_sems, sum_recv, fin_sems, fin_recv, out_sems,
):
    planes = bv.shape[1]
    rows = bv.shape[2]
    strip = rows // STRIPS
    z = lax.axis_index("depth")
    lat = lax.axis_index("lat")
    sub = lax.axis_index("sub")

    loads = []
    for t in range(2):
        loads.append(pltpu.make_async_copy(
            field.at[0, :, :, pl.ds(t * LANES, LANES)],
            fv.at[t, :, pl.ds(8, rows), :], load_sem.at[t]))
    for t in range(2):
        loads.append(pltpu.make_async_copy(
            bins.at[0, :, :, pl.ds(t * LANES, LANES)], bv.at[t], load_sem.at[2 + t]))
    for load in loads:
        load.start()

    barrier = pltpu.get_barrier_semaphore()
    pl.semaphore_signal(barrier, inc=1, device_id={"sub": 1 - sub}, device_id_type=MESH)
    has_up = lat > 0
    has_down = lat < n_lat - 1

    @pl.when(has_up)
    def _():
        pl.semaphore_signal(barrier, inc=1, device_id={"lat": lat - 1}, device_id_type=MESH)

    @pl.when(has_down)
    def _():
        pl.semaphore_signal(barrier, inc=1, device_id={"lat": lat + 1}, device_id_type=MESH)

    greet = 1 + has_up.astype(jnp.int32) + has_down.astype(jnp.int32)
    is_end = jnp.logical_or(z == 0, z == 3)
    is_mid = jnp.logical_not(is_end)
    left = z < 2
    near = jnp.where(z == 0, 1, jnp.where(z == 1, 0, jnp.where(z == 2, 3, 2)))
    peer = 3 - z
    across = jnp.where(z == 0, 2, jnp.where(z == 1, 3, jnp.where(z == 2, 0, 1)))
    if exchange:
        pl.semaphore_signal(barrier, inc=1, device_id={"depth": near}, device_id_type=MESH)
        pl.semaphore_signal(barrier, inc=1, device_id={"depth": across}, device_id_type=MESH)

        @pl.when(is_mid)
        def _():
            pl.semaphore_signal(barrier, inc=1, device_id={"depth": peer}, device_id_type=MESH)

        greet = greet + 2 + is_mid.astype(jnp.int32)

    lane = lax.broadcasted_iota(jnp.int32, (8, LANES), 1)
    first_lane = lane == 0
    last_lane = lane == LANES - 1

    table[...] = jnp.zeros_like(table)
    n_bins = color.shape[1]
    for c in range(3):
        table[c, :, 0:n_bins] = jnp.broadcast_to(color[c:c + 1, :], (8, n_bins))
    table[3, :, 0:n_bins] = jnp.broadcast_to(
        opacity[...].reshape(1, n_bins), (8, n_bins)) * (-1.0 / math.log(2.0))

    loads[0].wait()
    loads[1].wait()

    for t in range(2):
        for k in range(planes):
            row_send[0, t, k:k + 1, :] = fv[t, k + 1, 8:9, :]
            row_send[1, t, k:k + 1, :] = fv[t, k + 1, 7 + rows:8 + rows, :]

    pl.semaphore_wait(barrier, greet)

    up = pltpu.make_async_remote_copy(
        src_ref=row_send.at[0], dst_ref=row_recv.at[1], send_sem=row_sem.at[0],
        recv_sem=row_sem.at[2], device_id={"lat": lat - 1}, device_id_type=MESH)
    down = pltpu.make_async_remote_copy(
        src_ref=row_send.at[1], dst_ref=row_recv.at[0], send_sem=row_sem.at[1],
        recv_sem=row_sem.at[3], device_id={"lat": lat + 1}, device_id_type=MESH)

    @pl.when(has_up)
    def _():
        up.start()

    @pl.when(has_down)
    def _():
        down.start()

    def pack(src, offset):
        def chunk(i, _):
            r0 = pl.multiple_of(i * 8, 8)
            packed = jnp.zeros((8, LANES), jnp.float32)
            for k in range(planes):
                to = (2 * k + offset) % LANES
                shift = (to + 1) % LANES if src == 1 else to
                value = fv[src, k + 1, pl.ds(8 + r0, 8), :]
                if shift:
                    value = pltpu.roll(value, shift, 1)
                packed = jnp.where(lane == to, value, packed)
            col_send[pl.ds(r0, 8), :] = packed
            return 0
        lax.fori_loop(0, rows // 8, chunk, 0)

    @pl.when(sub == 0)
    def _():
        pack(1, 0)

    @pl.when(sub == 1)
    def _():
        pack(0, -1)

    side = pltpu.make_async_remote_copy(
        src_ref=col_send, dst_ref=col_recv, send_sem=col_sem.at[0],
        recv_sem=col_sem.at[1], device_id={"sub": 1 - sub}, device_id_type=MESH)
    side.start()

    @pl.when(has_up)
    def _():
        up.wait_send()
        down.wait_recv()

    @pl.when(has_down)
    def _():
        down.wait_send()
        up.wait_recv()

    @pl.when(jnp.logical_not(has_up))
    def _():
        row_recv[0] = jnp.zeros(row_recv.shape[1:], jnp.float32)

    @pl.when(jnp.logical_not(has_down))
    def _():
        row_recv[1] = jnp.zeros(row_recv.shape[1:], jnp.float32)

    for t in range(2):
        for k in range(planes):
            fv[t, k + 1, 7:8, :] = row_recv[0, t, k:k + 1, :]
            fv[t, k + 1, 8 + rows:9 + rows, :] = row_recv[1, t, k:k + 1, :]

    loads[2].wait()
    loads[3].wait()
    side.wait()

    lx = light[0] * 0.5
    ly = light[1] * 0.5
    lz = light[2] * 0.5
    count = counts[0, 0, 0]

    def march(r0):
        halo = col_recv[pl.ds(r0, 8), :]
        before = [fv[t, 0, pl.ds(8 + r0, 8), :] for t in range(2)]
        here = [fv[t, 1, pl.ds(8 + r0, 8), :] for t in range(2)]
        total = [[jnp.zeros((8, LANES), jnp.float32) for _ in range(3)] for _ in range(2)]
        remain = [jnp.ones((8, LANES), jnp.float32) for _ in range(2)]
        colors = [table[c] for c in range(3)]
        extinct = table[3]
        for k in range(planes):
            after = [fv[t, k + 2, pl.ds(8 + r0, 8), :] for t in range(2)]
            extinct_k = jnp.where(k < count, extinct, 0.0)
            up1 = [pltpu.roll(here[t], 1, 1) for t in range(2)]
            dn1 = [pltpu.roll(here[t], LANES - 1, 1) for t in range(2)]
            minus = [jnp.where(first_lane, halo, up1[0]), jnp.where(first_lane, up1[0], up1[1])]
            plus = [jnp.where(last_lane, dn1[1], dn1[0]), jnp.where(last_lane, halo, dn1[1])]
            for t in range(2):
                gx = fv[t, k + 1, pl.ds(9 + r0, 8), :] - fv[t, k + 1, pl.ds(7 + r0, 8), :]
                gy = plus[t] - minus[t]
                gz = after[t] - before[t]
                dot = gx * lx + gy * ly + gz * lz
                norm = gx * gx + gy * gy + (gz * gz + 4.0)
                shading = jnp.abs(dot * lax.rsqrt(norm)) + 0.25
                soft = jnp.log(1.0 + jnp.exp(here[t]))
                bin_ids = bv[t, k, pl.ds(r0, 8), :]
                survive = jnp.exp2(lookup(extinct_k, bin_ids) * soft)
                left_over = remain[t] * survive
                weight = (remain[t] - left_over) * shading
                for c in range(3):
                    total[t][c] = total[t][c] + weight * lookup(colors[c], bin_ids)
                remain[t] = left_over
            before, here = here, after
            halo = pltpu.roll(halo, LANES - 2, 1)
        for t in range(2):
            for c in range(3):
                part[c, pl.ds(r0, 8), t * LANES:(t + 1) * LANES] = total[t][c]
            part[3, pl.ds(r0, 8), t * LANES:(t + 1) * LANES] = remain[t]

    def compute(s):
        def group(i, _):
            march(pl.multiple_of(s * strip + i * 8, 8))
            return 0
        lax.fori_loop(0, strip // 8, group, 0)

    def at_rows(s):
        return pl.ds(pl.multiple_of(s * strip, strip), strip)

    def to_out(s, src):
        return pltpu.make_async_copy(
            src.at[:, at_rows(s), :], out.at[:, at_rows(s), :], out_sems.at[s])

    if not exchange:
        def plain(s, _):
            compute(s)
            to_out(s, part).start()
            return 0
        lax.fori_loop(0, STRIPS, plain, 0)

        def finish(s, _):
            to_out(s, part).wait()
            return 0
        lax.fori_loop(0, STRIPS, finish, 0)
        return

    def send_part(s):
        return pltpu.make_async_remote_copy(
            src_ref=part.at[:, at_rows(s), :], dst_ref=ends.at[:, at_rows(s), :],
            send_sem=part_sems.at[s], recv_sem=part_recv.at[s],
            device_id={"depth": near}, device_id_type=MESH)

    def send_far(s):
        return pltpu.make_async_remote_copy(
            src_ref=part.at[3, at_rows(s), :], dst_ref=far_remain.at[1, at_rows(s), :],
            send_sem=far_sems.at[s], recv_sem=far_recv.at[s],
            device_id={"depth": across}, device_id_type=MESH)

    def send_own(s):
        return pltpu.make_async_remote_copy(
            src_ref=part.at[3, at_rows(s), :], dst_ref=far_remain.at[0, at_rows(s), :],
            send_sem=own_sems.at[s], recv_sem=own_recv.at[s],
            device_id={"depth": peer}, device_id_type=MESH)

    def send_sum(s):
        return pltpu.make_async_remote_copy(
            src_ref=mine.at[:, at_rows(s), :], dst_ref=theirs.at[:, at_rows(s), :],
            send_sem=sum_sems.at[s], recv_sem=sum_recv.at[s],
            device_id={"depth": peer}, device_id_type=MESH)

    def send_fin(s):
        return pltpu.make_async_remote_copy(
            src_ref=fin.at[:, at_rows(s), :], dst_ref=out.at[:, at_rows(s), :],
            send_sem=fin_sems.at[s], recv_sem=fin_recv.at[s],
            device_id={"depth": near}, device_id_type=MESH)

    @pl.when(is_end)
    def _():
        def first(s, _):
            compute(s)
            send_far(s).start()
            send_part(s).start()
            return 0
        lax.fori_loop(0, STRIPS, first, 0)

        def last(s, _):
            send_far(s).wait_send()
            send_part(s).wait_send()
            send_fin(s).wait_recv()
            return 0
        lax.fori_loop(0, STRIPS, last, 0)

    def rank_of(brick):
        rank = jnp.int32(0)
        for r in range(1, n_depth):
            rank = rank + jnp.where(order[r] == brick, r, 0)
        return rank

    rank_mine = rank_of(z)
    rank_near = rank_of(near)
    rank_peer = rank_of(peer)
    rank_across = rank_of(across)

    def sums(s):
        def group(i, _):
            r = pl.ds(pl.multiple_of(s * strip + i * 8, 8), 8)
            one = jnp.ones((8, part.shape[2]), jnp.float32)
            own = part[3, r, :]
            end = ends[3, r, :]
            there = far_remain[0, r, :]
            far = far_remain[1, r, :]

            def gate(a, b, value):
                return jnp.where(a < b, value, one)

            w_own = (gate(rank_near, rank_mine, end) * gate(rank_peer, rank_mine, there)
                     * gate(rank_across, rank_mine, far))
            w_end = (gate(rank_mine, rank_near, own) * gate(rank_peer, rank_near, there)
                     * gate(rank_across, rank_near, far))
            for c in range(3):
                mine[c, r, :] = w_own * part[c, r, :] + w_end * ends[c, r, :]
            fin[3, r, :] = 1.0 - (own * end) * (there * far)
            return 0
        lax.fori_loop(0, strip // 8, group, 0)

    def done(s):
        def group(i, _):
            r = pl.ds(pl.multiple_of(s * strip + i * 8, 8), 8)
            for c in range(3):
                fin[c, r, :] = mine[c, r, :] + theirs[c, r, :]
            return 0
        lax.fori_loop(0, strip // 8, group, 0)

    @pl.when(is_mid)
    def _():
        def stage(it, _):
            @pl.when(it < STRIPS)
            def _():
                compute(it)
                send_own(it).start()

            @pl.when(jnp.logical_and(it >= LAG_SUM, it < STRIPS + LAG_SUM))
            def _():
                s = it - LAG_SUM
                send_part(s).wait_recv()
                send_far(s).wait_recv()
                send_own(s).wait_recv()
                sums(s)
                send_sum(s).start()

            @pl.when(it >= LAG_DONE)
            def _():
                s = it - LAG_DONE
                send_sum(s).wait_recv()
                done(s)
                send_fin(s).start()
                to_out(s, fin).start()
            return 0
        lax.fori_loop(0, STRIPS + LAG_DONE, stage, 0)

        def last(s, _):
            send_own(s).wait_send()
            send_sum(s).wait_send()
            send_fin(s).wait_send()
            to_out(s, fin).wait()
            return 0
        lax.fori_loop(0, STRIPS, last, 0)


def on_device(n_depth, n_lat, scalar_field, bin_index, sample_counts, view_order, light_dir,
              tf_color, tf_opacity):
    exchange = n_depth == 4
    planes, rows, cols = bin_index.shape[1:]
    image = (4, rows, cols)
    dma = pltpu.SemaphoreType.DMA
    smem = pl.BlockSpec(memory_space=pltpu.SMEM)
    vmem = pl.BlockSpec(memory_space=pltpu.VMEM)
    hbm = pl.BlockSpec(memory_space=pl.ANY)
    f32 = jnp.float32
    result = pl.pallas_call(
        functools.partial(kernel, n_depth, n_lat, exchange),
        out_shape=jax.ShapeDtypeStruct(image, f32),
        in_specs=[hbm, hbm, smem, smem, smem, vmem, vmem],
        out_specs=hbm,
        scratch_shapes=[
            pltpu.VMEM((2, planes + 2, rows + 16, LANES), f32),
            pltpu.VMEM((2, planes, rows, LANES), jnp.int32),
            pltpu.VMEM((rows, LANES), f32),
            pltpu.VMEM((rows, LANES), f32),
            pltpu.VMEM((2, 2, planes, LANES), f32),
            pltpu.VMEM((2, 2, planes, LANES), f32),
            pltpu.VMEM((4, 8, LANES), f32),
            pltpu.VMEM(image, f32),
            pltpu.VMEM(image, f32),
            pltpu.VMEM((2, rows, cols), f32),
            pltpu.VMEM((3, rows, cols), f32),
            pltpu.VMEM((3, rows, cols), f32),
            pltpu.VMEM(image, f32),
            dma((4,)), dma((2,)), dma((4,)), dma((1,)),
        ] + [dma((STRIPS,))] * 11,
        compiler_params=pltpu.CompilerParams(
            collective_id=0, has_side_effects=True, vmem_limit_bytes=48 * 1024 * 1024),
    )(scalar_field, bin_index, sample_counts, view_order, light_dir, tf_color, tf_opacity)
    if exchange:
        return result
    return composite(lax.all_gather(result[None], "depth", axis=0, tiled=True), view_order)


def solution(mesh):
    return jax.shard_map(
        functools.partial(on_device, mesh.shape["depth"], mesh.shape["lat"]),
        mesh=mesh,
        in_specs=(
            P(("groups", "depth"), None, "lat", "sub"),
            P(("groups", "depth"), None, "lat", "sub"),
            P(("groups", "depth"), "lat", "sub"),
            P("groups"),
            P(),
            P(),
            P(),
        ),
        out_specs=P(None, ("groups", "lat"), "sub"),
        check_vma=False,
    )
```

time: 291 us -> 65.2 us (0.22)
  waiting for transfers between devices: 122 us -> 0 us
  other arithmetic: 77.3 us -> 0 us
  Pallas kernels: 0 us -> 58.6 us
  local copies, waits for them, and re-layouts: 48 us -> 5.8 us
  loops' own time: 16.4 us -> 0 us
  between operations: 15.5 us -> 0.67 us
  starting transfers between devices: 8.89 us -> 0 us
    all_gather x1 -> x0, waiting for transfers between devices: 122 us -> none  [on_device(): all_parts = lax.all_gather(partial_value, 'depth', axis=0, tiled=True)]
    pallas_call x0 -> x1, Pallas kernels: none -> 58.6 us  [on_device(): pl.pallas_call(functools.partial(kernel, n_depth, n_lat, exchange), out_s...]
    reduce_sum x11 -> x0, other arithmetic: 33.1 us -> none  [one_plane(): jnp.sum(jnp.where(choose, tf_table[:, :, None, None], 0.0), axis=1)]
    another operation x2 -> x0, loops' own time: 16.4 us -> none  [the longest x1 8.56 us: on_device(): accum_rgb, remain = lax.fori_loop(0, sample_count, one_plane, init)]
    squeeze x11 -> x0, local copies, waits for them, and re-layouts: 14.6 us -> none  [shading_terms(): lax.dynamic_index_in_dim(padded, depth_step + 1, 0, keepdims=False)]
    eq x11 -> x0, other arithmetic: 13.3 us -> none  [one_plane(): choose = bins_plane[None, None] == bin_ids[None, :, None, None]]
    mul x15 -> x0, other arithmetic: 11.5 us -> none  [the longest x11 7.42 us: one_plane(): return (accum_rgb, remain * survive)]
    eq x11 -> x0, local copies, waits for them, and re-layouts: 10.7 us -> none  [one_plane(): choose = bins_plane[None, None] == bin_ids[None, :, None, None]]
  transfers between devices with their start and end apart: 5 -> 0, of which waited for: 1 -> 0; matrix products, arithmetic and copies ran while one was open for 3% -> 0% of each run, Pallas kernels for 0% -> 0%
where the time goes in v1:
time: 65.2 us; the launch traced here: 65 us
  Pallas kernels  58.6 us (90%)
  local copies, waits for them, and re-layouts  5.8 us (9%)
  between operations  0.67 us (1%)
    pallas_call x1, Pallas kernels, on_device(): pl.pallas_call(functools.partial(kernel, n_depth, n_lat, exchange), out_s...  58.6 us
    unnamed x11, local copies, waits for them, and re-layouts  5.8 us

profile of v1, /device:TPU:0, one launch (start us, length us, event | category | flops | bytes accessed | tf_op | source)
XLA Modules:
  0.0 65.0 jit_solution(17216520371299083796)
XLA Ops:
  0.7 0.0 copy-start
  0.7 2.2 %copy-done = s32[1,16,256,256]{3,2,1,0:T(8,128)S(1)} copy-done((s32[1,16,256,256]{3,2,1,0:T(8,128)S(1)}, s32[1,16,256,256]{3,2,1,0:T(8,128)}, u32[]{:S(2)}) %copy-start) | copy-done | bytes 4194328
  2.8 0.0 copy-start.1
  2.8 0.7 %copy-done.1 = f32[3,32]{1,0:T(4,128)S(1)} copy-done((f32[3,32]{1,0:T(4,128)S(1)}, f32[3,32]{1,0:T(4,128)}, u32[]{:S(2)}) %copy-start.1) | copy-done | bytes 408
  3.5 0.0 copy-start.2
  3.5 0.7 %copy-done.2 = s32[4]{0:T(128)S(1)} copy-done((s32[4]{0:T(128)S(1)}, s32[4]{0:T(128)}, u32[]{:S(2)}) %copy-start.2) | copy-done | bytes 40
  4.2 0.0 copy-start.3
  4.2 0.7 %copy-done.3 = f32[3]{0:T(128)S(1)} copy-done((f32[3]{0:T(128)S(1)}, f32[3]{0:T(128)}, u32[]{:S(2)}) %copy-start.3) | copy-done | bytes 36
  4.8 0.0 copy-start.4
  4.8 0.7 %copy-done.4 = f32[32]{0:T(128)S(1)} copy-done((f32[32]{0:T(128)S(1)}, f32[32]{0:T(128)}, u32[]{:S(2)}) %copy-start.4) | copy-done | bytes 152
  5.5 58.6 %shard_map.73 = f32[4,256,256]{2,1,0:T(8,128)S(1)} custom-call(f32[1,18,256,256]{3,2,1,0:T(8,128)} %field.1, s32[1,16,256,256]{3,2,1,0:T(8,128)S(1)} %copy-done, s32[1,1,1]{2,1,0:T(1,128)S(6)} %copy.9.counts, s32[4]{0:T(128)S(1)} %copy-done.2, f32[3]{0:T(128)S(1)} %copy-done.3, f32[3,32]{1,0:T(4,128)S(1)} %copy-done.1, f32[32]{0:T(128)S(1)} %copy-done.4), custom_call_target="tpu_custom_call" | custom-call | tf_op jit(solution)/shard_map/pallas_call | solution.py:386
  64.1 1.0 %copy.10 = f32[4,256,256]{2,1,0:T(8,128)} copy(f32[4,256,256]{2,1,0:T(8,128)S(1)} %shard_map.73) | data formatting | bytes 2097152
Async XLA Ops:
  0.7 2.2 %copy-start = (s32[1,16,256,256]{3,2,1,0:T(8,128)S(1)}, s32[1,16,256,256]{3,2,1,0:T(8,128)}, u32[]{:S(2)}) copy-start(s32[1,16,256,256]{3,2,1,0:T(8,128)} %bins.1) | copy-start | bytes 12582916
  2.8 0.7 %copy-start.1 = (f32[3,32]{1,0:T(4,128)S(1)}, f32[3,32]{1,0:T(4,128)}, u32[]{:S(2)}) copy-start(f32[3,32]{1,0:T(4,128)} %color.1) | copy-start | bytes 1156
  3.5 0.7 %copy-start.2 = (s32[4]{0:T(128)S(1)}, s32[4]{0:T(128)}, u32[]{:S(2)}) copy-start(s32[4]{0:T(128)} %order.1) | copy-start | bytes 52
  4.2 0.7 %copy-start.3 = (f32[3]{0:T(128)S(1)}, f32[3]{0:T(128)}, u32[]{:S(2)}) copy-start(f32[3]{0:T(128)} %light.1) | copy-start | bytes 40
  4.8 0.7 %copy-start.4 = (f32[32]{0:T(128)S(1)}, f32[32]{0:T(128)}, u32[]{:S(2)}) copy-start(f32[32]{0:T(128)} %opacity.1) | copy-start | bytes 388

commit v2 on v1

--- a/solution.py
+++ b/solution.py
@@ -10,9 +10,9 @@
 
 MESH = pl.DeviceIdType.MESH
 LANES = 128
-STRIPS = 8
-LAG_SUM = 1
-LAG_DONE = 2
+STRIPS = 16
+CHUNKS = 4
+LAG_DONE = 3
 
 
 def composite(stacked, view_order):
@@ -36,12 +36,12 @@
 
 def kernel(
     n_depth, n_lat, exchange,
-    field, bins, counts, order, light, color, opacity, out,
-    fv, bv, col_send, col_recv, row_send, row_recv, table,
+    field, bins, counts_in, order_in, light_in, color_in, opacity_in, out,
+    counts, order, light, color, opacity, small_sem, fv, bv, col_send, col_recv, row_send, row_recv, table,
     part, ends, far_remain, mine, theirs, fin,
-    load_sem, col_sem, row_sem, barrier_pad,
-    part_sems, part_recv, own_sems, own_recv, far_sems, far_recv,
-    sum_sems, sum_recv, fin_sems, fin_recv, out_sems,
+    load_sem, col_sem, row_sem,
+    part_sems, part_recv, own_sems, own_recv, end_sems, end_recv, far_sems, far_recv,
+    sum_sems, sum_recv, opac_sems, opac_recv, fin_sems, fin_recv, out_sems, out_opac_sems,
 ):
     planes = bv.shape[1]
     rows = bv.shape[2]
@@ -50,14 +50,25 @@
     lat = lax.axis_index("lat")
     sub = lax.axis_index("sub")
 
+    small = [
+        pltpu.make_async_copy(src, dst, small_sem.at[i])
+        for i, (src, dst) in enumerate((
+            (counts_in, counts), (order_in, order), (light_in, light),
+            (color_in, color), (opacity_in, opacity)))
+    ]
+    for load in small:
+        load.start()
+
+    chunk_rows = rows // CHUNKS
     loads = []
-    for t in range(2):
-        loads.append(pltpu.make_async_copy(
-            field.at[0, :, :, pl.ds(t * LANES, LANES)],
-            fv.at[t, :, pl.ds(8, rows), :], load_sem.at[t]))
-    for t in range(2):
-        loads.append(pltpu.make_async_copy(
-            bins.at[0, :, :, pl.ds(t * LANES, LANES)], bv.at[t], load_sem.at[2 + t]))
+    for c in range(CHUNKS):
+        for t in range(2):
+            loads.append(pltpu.make_async_copy(
+                field.at[0, :, pl.ds(c * chunk_rows, chunk_rows), pl.ds(t * LANES, LANES)],
+                fv.at[t, :, pl.ds(8 + c * chunk_rows, chunk_rows), :], load_sem.at[c, t]))
+            loads.append(pltpu.make_async_copy(
+                bins.at[0, :, pl.ds(c * chunk_rows, chunk_rows), pl.ds(t * LANES, LANES)],
+                bv.at[t, :, pl.ds(c * chunk_rows, chunk_rows), :], load_sem.at[c, 2 + t]))
     for load in loads:
         load.start()
 
@@ -77,24 +88,24 @@
     greet = 1 + has_up.astype(jnp.int32) + has_down.astype(jnp.int32)
     is_end = jnp.logical_or(z == 0, z == 3)
     is_mid = jnp.logical_not(is_end)
-    left = z < 2
     near = jnp.where(z == 0, 1, jnp.where(z == 1, 0, jnp.where(z == 2, 3, 2)))
     peer = 3 - z
-    across = jnp.where(z == 0, 2, jnp.where(z == 1, 3, jnp.where(z == 2, 0, 1)))
+    across = 3 - near
     if exchange:
         pl.semaphore_signal(barrier, inc=1, device_id={"depth": near}, device_id_type=MESH)
-        pl.semaphore_signal(barrier, inc=1, device_id={"depth": across}, device_id_type=MESH)
 
         @pl.when(is_mid)
         def _():
             pl.semaphore_signal(barrier, inc=1, device_id={"depth": peer}, device_id_type=MESH)
 
-        greet = greet + 2 + is_mid.astype(jnp.int32)
+        greet = greet + 1 + is_mid.astype(jnp.int32)
 
     lane = lax.broadcasted_iota(jnp.int32, (8, LANES), 1)
     first_lane = lane == 0
     last_lane = lane == LANES - 1
 
+    for load in small:
+        load.wait()
     table[...] = jnp.zeros_like(table)
     n_bins = color.shape[1]
     for c in range(3):
@@ -102,15 +113,66 @@
     table[3, :, 0:n_bins] = jnp.broadcast_to(
         opacity[...].reshape(1, n_bins), (8, n_bins)) * (-1.0 / math.log(2.0))
 
-    loads[0].wait()
-    loads[1].wait()
+    count = counts[0, 0, 0]
+
+    def at_rows(s):
+        return pl.ds(pl.multiple_of(s * strip, strip), strip)
+
+    def send_own(s):
+        return pltpu.make_async_remote_copy(
+            src_ref=part.at[3, at_rows(s), :], dst_ref=far_remain.at[0, at_rows(s), :],
+            send_sem=own_sems.at[s], recv_sem=own_recv.at[s],
+            device_id={"depth": peer}, device_id_type=MESH)
+
+    def send_end(s):
+        return pltpu.make_async_remote_copy(
+            src_ref=part.at[3, at_rows(s), :], dst_ref=ends.at[3, at_rows(s), :],
+            send_sem=end_sems.at[s], recv_sem=end_recv.at[s],
+            device_id={"depth": near}, device_id_type=MESH)
+
+    def send_far(s):
+        return pltpu.make_async_remote_copy(
+            src_ref=ends.at[3, at_rows(s), :], dst_ref=far_remain.at[1, at_rows(s), :],
+            send_sem=far_sems.at[s], recv_sem=far_recv.at[s],
+            device_id={"depth": peer}, device_id_type=MESH)
+
+    def survive_all(s, _):
+        def group(i, _):
+            r0 = pl.multiple_of(s * strip + i * 8, 8)
+            for t in range(2):
+                power = jnp.zeros((8, LANES), jnp.float32)
+                for k in range(planes):
+                    extinct_k = jnp.where(k < count, table[3], 0.0)
+                    soft = jnp.log(1.0 + jnp.exp(fv[t, k + 1, pl.ds(8 + r0, 8), :]))
+                    power = power + lookup(extinct_k, bv[t, k, pl.ds(r0, 8), :]) * soft
+                part[3, pl.ds(r0, 8), t * LANES:(t + 1) * LANES] = jnp.exp2(power)
+            return 0
+        lax.fori_loop(0, strip // 8, group, 0)
+        if exchange:
+            @pl.when(is_end)
+            def _():
+                send_end(s).start()
+
+            @pl.when(is_mid)
+            def _():
+                send_own(s).start()
+        return 0
+
+    def remains(c):
+        for load in loads[4 * c:4 * c + 4]:
+            load.wait()
+        lax.fori_loop(c * STRIPS // CHUNKS, (c + 1) * STRIPS // CHUNKS, survive_all, 0)
+
+    pl.semaphore_wait(barrier, greet)
+    for c in range(CHUNKS // 2):
+        remains(c)
+    for load in loads[2 * CHUNKS:]:
+        load.wait()
 
     for t in range(2):
         for k in range(planes):
             row_send[0, t, k:k + 1, :] = fv[t, k + 1, 8:9, :]
             row_send[1, t, k:k + 1, :] = fv[t, k + 1, 7 + rows:8 + rows, :]
-
-    pl.semaphore_wait(barrier, greet)
 
     up = pltpu.make_async_remote_copy(
         src_ref=row_send.at[0], dst_ref=row_recv.at[1], send_sem=row_sem.at[0],
@@ -155,6 +217,9 @@
         recv_sem=col_sem.at[1], device_id={"sub": 1 - sub}, device_id_type=MESH)
     side.start()
 
+    for c in range(CHUNKS // 2, CHUNKS):
+        lax.fori_loop(c * STRIPS // CHUNKS, (c + 1) * STRIPS // CHUNKS, survive_all, 0)
+
     @pl.when(has_up)
     def _():
         up.wait_send()
@@ -178,14 +243,20 @@
             fv[t, k + 1, 7:8, :] = row_recv[0, t, k:k + 1, :]
             fv[t, k + 1, 8 + rows:9 + rows, :] = row_recv[1, t, k:k + 1, :]
 
-    loads[2].wait()
-    loads[3].wait()
+    if exchange:
+        @pl.when(is_mid)
+        def _():
+            def forward(s, _):
+                send_end(s).wait_recv()
+                send_far(s).start()
+                return 0
+            lax.fori_loop(0, STRIPS, forward, 0)
+
     side.wait()
 
     lx = light[0] * 0.5
     ly = light[1] * 0.5
     lz = light[2] * 0.5
-    count = counts[0, 0, 0]
 
     def march(r0):
         halo = col_recv[pl.ds(r0, 8), :]
@@ -200,8 +271,9 @@
             extinct_k = jnp.where(k < count, extinct, 0.0)
             up1 = [pltpu.roll(here[t], 1, 1) for t in range(2)]
             dn1 = [pltpu.roll(here[t], LANES - 1, 1) for t in range(2)]
-            minus = [jnp.where(first_lane, halo, up1[0]), jnp.where(first_lane, up1[0], up1[1])]
-            plus = [jnp.where(last_lane, dn1[1], dn1[0]), jnp.where(last_lane, halo, dn1[1])]
+            edge = pltpu.roll(halo, (LANES - 2 * k) % LANES, 1) if k else halo
+            minus = [jnp.where(first_lane, edge, up1[0]), jnp.where(first_lane, up1[0], up1[1])]
+            plus = [jnp.where(last_lane, dn1[1], dn1[0]), jnp.where(last_lane, edge, dn1[1])]
             for t in range(2):
                 gx = fv[t, k + 1, pl.ds(9 + r0, 8), :] - fv[t, k + 1, pl.ds(7 + r0, 8), :]
                 gy = plus[t] - minus[t]
@@ -218,20 +290,15 @@
                     total[t][c] = total[t][c] + weight * lookup(colors[c], bin_ids)
                 remain[t] = left_over
             before, here = here, after
-            halo = pltpu.roll(halo, LANES - 2, 1)
         for t in range(2):
             for c in range(3):
                 part[c, pl.ds(r0, 8), t * LANES:(t + 1) * LANES] = total[t][c]
-            part[3, pl.ds(r0, 8), t * LANES:(t + 1) * LANES] = remain[t]
 
     def compute(s):
         def group(i, _):
             march(pl.multiple_of(s * strip + i * 8, 8))
             return 0
         lax.fori_loop(0, strip // 8, group, 0)
-
-    def at_rows(s):
-        return pl.ds(pl.multiple_of(s * strip, strip), strip)
 
     def to_out(s, src):
         return pltpu.make_async_copy(
@@ -252,21 +319,9 @@
 
     def send_part(s):
         return pltpu.make_async_remote_copy(
-            src_ref=part.at[:, at_rows(s), :], dst_ref=ends.at[:, at_rows(s), :],
+            src_ref=part.at[0:3, at_rows(s), :], dst_ref=ends.at[0:3, at_rows(s), :],
             send_sem=part_sems.at[s], recv_sem=part_recv.at[s],
             device_id={"depth": near}, device_id_type=MESH)
-
-    def send_far(s):
-        return pltpu.make_async_remote_copy(
-            src_ref=part.at[3, at_rows(s), :], dst_ref=far_remain.at[1, at_rows(s), :],
-            send_sem=far_sems.at[s], recv_sem=far_recv.at[s],
-            device_id={"depth": across}, device_id_type=MESH)
-
-    def send_own(s):
-        return pltpu.make_async_remote_copy(
-            src_ref=part.at[3, at_rows(s), :], dst_ref=far_remain.at[0, at_rows(s), :],
-            send_sem=own_sems.at[s], recv_sem=own_recv.at[s],
-            device_id={"depth": peer}, device_id_type=MESH)
 
     def send_sum(s):
         return pltpu.make_async_remote_copy(
@@ -276,22 +331,36 @@
 
     def send_fin(s):
         return pltpu.make_async_remote_copy(
-            src_ref=fin.at[:, at_rows(s), :], dst_ref=out.at[:, at_rows(s), :],
+            src_ref=fin.at[0:3, at_rows(s), :], dst_ref=out.at[0:3, at_rows(s), :],
             send_sem=fin_sems.at[s], recv_sem=fin_recv.at[s],
             device_id={"depth": near}, device_id_type=MESH)
 
+    def send_opac(s):
+        return pltpu.make_async_remote_copy(
+            src_ref=fin.at[3, at_rows(s), :], dst_ref=out.at[3, at_rows(s), :],
+            send_sem=opac_sems.at[s], recv_sem=opac_recv.at[s],
+            device_id={"depth": near}, device_id_type=MESH)
+
+    def rgb_out(s):
+        return pltpu.make_async_copy(
+            fin.at[0:3, at_rows(s), :], out.at[0:3, at_rows(s), :], out_sems.at[s])
+
+    def opac_out(s):
+        return pltpu.make_async_copy(
+            fin.at[3, at_rows(s), :], out.at[3, at_rows(s), :], out_opac_sems.at[s])
+
     @pl.when(is_end)
     def _():
         def first(s, _):
             compute(s)
-            send_far(s).start()
             send_part(s).start()
             return 0
         lax.fori_loop(0, STRIPS, first, 0)
 
         def last(s, _):
-            send_far(s).wait_send()
+            send_end(s).wait_send()
             send_part(s).wait_send()
+            send_opac(s).wait_recv()
             send_fin(s).wait_recv()
             return 0
         lax.fori_loop(0, STRIPS, last, 0)
@@ -307,35 +376,27 @@
     rank_peer = rank_of(peer)
     rank_across = rank_of(across)
 
+    def gate(a, b, value):
+        return jnp.where(a < b, value, jnp.ones_like(value))
+
     def sums(s):
-        def group(i, _):
-            r = pl.ds(pl.multiple_of(s * strip + i * 8, 8), 8)
-            one = jnp.ones((8, part.shape[2]), jnp.float32)
-            own = part[3, r, :]
-            end = ends[3, r, :]
-            there = far_remain[0, r, :]
-            far = far_remain[1, r, :]
-
-            def gate(a, b, value):
-                return jnp.where(a < b, value, one)
-
-            w_own = (gate(rank_near, rank_mine, end) * gate(rank_peer, rank_mine, there)
-                     * gate(rank_across, rank_mine, far))
-            w_end = (gate(rank_mine, rank_near, own) * gate(rank_peer, rank_near, there)
-                     * gate(rank_across, rank_near, far))
-            for c in range(3):
-                mine[c, r, :] = w_own * part[c, r, :] + w_end * ends[c, r, :]
-            fin[3, r, :] = 1.0 - (own * end) * (there * far)
-            return 0
-        lax.fori_loop(0, strip // 8, group, 0)
+        r = at_rows(s)
+        own = part[3, r, :]
+        end = ends[3, r, :]
+        there = far_remain[0, r, :]
+        far = far_remain[1, r, :]
+        w_own = (gate(rank_near, rank_mine, end) * gate(rank_peer, rank_mine, there)
+                 * gate(rank_across, rank_mine, far))
+        w_end = (gate(rank_mine, rank_near, own) * gate(rank_peer, rank_near, there)
+                 * gate(rank_across, rank_near, far))
+        for c in range(3):
+            mine[c, r, :] = w_own * part[c, r, :] + w_end * ends[c, r, :]
+        fin[3, r, :] = 1.0 - (own * end) * (there * far)
 
     def done(s):
-        def group(i, _):
-            r = pl.ds(pl.multiple_of(s * strip + i * 8, 8), 8)
-            for c in range(3):
-                fin[c, r, :] = mine[c, r, :] + theirs[c, r, :]
-            return 0
-        lax.fori_loop(0, strip // 8, group, 0)
+        r = at_rows(s)
+        for c in range(3):
+            fin[c, r, :] = mine[c, r, :] + theirs[c, r, :]
 
     @pl.when(is_mid)
     def _():
@@ -343,16 +404,13 @@
             @pl.when(it < STRIPS)
             def _():
                 compute(it)
-                send_own(it).start()
-
-            @pl.when(jnp.logical_and(it >= LAG_SUM, it < STRIPS + LAG_SUM))
-            def _():
-                s = it - LAG_SUM
-                send_part(s).wait_recv()
-                send_far(s).wait_recv()
-                send_own(s).wait_recv()
-                sums(s)
-                send_sum(s).start()
+                send_part(it).wait_recv()
+                send_far(it).wait_recv()
+                send_own(it).wait_recv()
+                sums(it)
+                send_sum(it).start()
+                send_opac(it).start()
+                opac_out(it).start()
 
             @pl.when(it >= LAG_DONE)
             def _():
@@ -360,15 +418,18 @@
                 send_sum(s).wait_recv()
                 done(s)
                 send_fin(s).start()
-                to_out(s, fin).start()
+                rgb_out(s).start()
             return 0
         lax.fori_loop(0, STRIPS + LAG_DONE, stage, 0)
 
         def last(s, _):
             send_own(s).wait_send()
+            send_far(s).wait_send()
             send_sum(s).wait_send()
+            send_opac(s).wait_send()
             send_fin(s).wait_send()
-            to_out(s, fin).wait()
+            opac_out(s).wait()
+            rgb_out(s).wait()
             return 0
         lax.fori_loop(0, STRIPS, last, 0)
 
@@ -379,16 +440,20 @@
     planes, rows, cols = bin_index.shape[1:]
     image = (4, rows, cols)
     dma = pltpu.SemaphoreType.DMA
-    smem = pl.BlockSpec(memory_space=pltpu.SMEM)
-    vmem = pl.BlockSpec(memory_space=pltpu.VMEM)
-    hbm = pl.BlockSpec(memory_space=pl.ANY)
+    hbm = pl.BlockSpec(memory_space=pltpu.HBM)
     f32 = jnp.float32
     result = pl.pallas_call(
         functools.partial(kernel, n_depth, n_lat, exchange),
         out_shape=jax.ShapeDtypeStruct(image, f32),
-        in_specs=[hbm, hbm, smem, smem, smem, vmem, vmem],
-        out_specs=hbm,
+        in_specs=[hbm] * 7,
+        out_specs=pl.BlockSpec(memory_space=pl.ANY),
         scratch_shapes=[
+            pltpu.SMEM(sample_counts.shape, jnp.int32),
+            pltpu.SMEM(view_order.shape, jnp.int32),
+            pltpu.SMEM(light_dir.shape, f32),
+            pltpu.VMEM(tf_color.shape, f32),
+            pltpu.VMEM(tf_opacity.shape, f32),
+            dma((5,)),
             pltpu.VMEM((2, planes + 2, rows + 16, LANES), f32),
             pltpu.VMEM((2, planes, rows, LANES), jnp.int32),
             pltpu.VMEM((rows, LANES), f32),
@@ -402,10 +467,10 @@
             pltpu.VMEM((3, rows, cols), f32),
             pltpu.VMEM((3, rows, cols), f32),
             pltpu.VMEM(image, f32),
-            dma((4,)), dma((2,)), dma((4,)), dma((1,)),
-        ] + [dma((STRIPS,))] * 11,
+            dma((CHUNKS, 4)), dma((2,)), dma((4,)),
+        ] + [dma((STRIPS,))] * 16,
         compiler_params=pltpu.CompilerParams(
-            collective_id=0, has_side_effects=True, vmem_limit_bytes=48 * 1024 * 1024),
+            collective_id=0, has_side_effects=True, vmem_limit_bytes=60 * 1024 * 1024),
     )(scalar_field, bin_index, sample_counts, view_order, light_dir, tf_color, tf_opacity)
     if exchange:
         return result

time: 65.2 us -> 50.2 us (0.77)
  Pallas kernels: 58.6 us -> 47.1 us
  local copies, waits for them, and re-layouts: 5.8 us -> 2.29 us
    pallas_call x1, Pallas kernels: 58.6 us -> 47.1 us  [on_device(): pl.pallas_call(functools.partial(kernel, n_depth, n_lat, exchange), out_s...]
    unnamed x11 -> x1, local copies, waits for them, and re-layouts: 5.8 us -> 2.29 us
where the time goes in v2:
time: 50.2 us; the launch traced here: 50.1 us
  Pallas kernels  47.1 us (94%)
  local copies, waits for them, and re-layouts  2.29 us (5%)
  between operations  0.66 us (1%)
    pallas_call x1, Pallas kernels, on_device(): pl.pallas_call(functools.partial(kernel, n_depth, n_lat, exchange), out_s...  47.1 us
    unnamed x1, local copies, waits for them, and re-layouts  2.29 us

profile of v2, /device:TPU:0, one launch (start us, length us, event | category | flops | bytes accessed | tf_op | source)
XLA Modules:
  0.0 50.1 jit_solution(4519801023439702381)
XLA Ops:
  0.7 47.1 %shard_map.73 = f32[4,256,256]{2,1,0:T(8,128)} custom-call(f32[1,18,256,256]{3,2,1,0:T(8,128)} %field.1, s32[1,16,256,256]{3,2,1,0:T(8,128)} %bins.1, s32[1,1,1]{2,1,0:T(1,128)S(6)} %copy.9.counts_in, s32[4]{0:T(128)} %order_in.1, f32[3]{0:T(128)} %light_in.1, f32[3,32]{1,0:T(4,128)} %color_in.1, f32[32]{0:T(128)} %opacity_in.1), custom_call_target="tpu_custom_call" | custom-call | tf_op jit(solution)/shard_map/pallas_call | solution.py:445
  47.8 2.3 %copy.10 = f32[4,256,256]{2,1,0:T(8,128)} copy(f32[4,256,256]{2,1,0:T(8,128)} %shard_map.73) | data formatting | bytes 2097152

commit v3 on v2

--- a/solution.py
+++ b/solution.py
@@ -12,7 +12,7 @@
 LANES = 128
 STRIPS = 16
 CHUNKS = 4
-LAG_DONE = 3
+LAG_DONE = 4
 
 
 def composite(stacked, view_order):
@@ -101,6 +101,7 @@
         greet = greet + 1 + is_mid.astype(jnp.int32)
 
     lane = lax.broadcasted_iota(jnp.int32, (8, LANES), 1)
+    wide_lane = lax.broadcasted_iota(jnp.int32, (32, LANES), 1)
     first_lane = lane == 0
     last_lane = lane == LANES - 1
 
@@ -191,18 +192,18 @@
 
     def pack(src, offset):
         def chunk(i, _):
-            r0 = pl.multiple_of(i * 8, 8)
-            packed = jnp.zeros((8, LANES), jnp.float32)
+            r0 = pl.multiple_of(i * 32, 32)
+            packed = jnp.zeros((32, LANES), jnp.float32)
             for k in range(planes):
                 to = (2 * k + offset) % LANES
                 shift = (to + 1) % LANES if src == 1 else to
-                value = fv[src, k + 1, pl.ds(8 + r0, 8), :]
+                value = fv[src, k + 1, pl.ds(8 + r0, 32), :]
                 if shift:
                     value = pltpu.roll(value, shift, 1)
-                packed = jnp.where(lane == to, value, packed)
-            col_send[pl.ds(r0, 8), :] = packed
-            return 0
-        lax.fori_loop(0, rows // 8, chunk, 0)
+                packed = jnp.where(wide_lane == to, value, packed)
+            col_send[pl.ds(r0, 32), :] = packed
+            return 0
+        lax.fori_loop(0, rows // 32, chunk, 0)
 
     @pl.when(sub == 0)
     def _():
@@ -242,15 +243,6 @@
         for k in range(planes):
             fv[t, k + 1, 7:8, :] = row_recv[0, t, k:k + 1, :]
             fv[t, k + 1, 8 + rows:9 + rows, :] = row_recv[1, t, k:k + 1, :]
-
-    if exchange:
-        @pl.when(is_mid)
-        def _():
-            def forward(s, _):
-                send_end(s).wait_recv()
-                send_far(s).start()
-                return 0
-            lax.fori_loop(0, STRIPS, forward, 0)
 
     side.wait()
 
@@ -391,7 +383,7 @@
                  * gate(rank_across, rank_near, far))
         for c in range(3):
             mine[c, r, :] = w_own * part[c, r, :] + w_end * ends[c, r, :]
-        fin[3, r, :] = 1.0 - (own * end) * (there * far)
+        fin[3, r, :] = (own * end) * (there * far)
 
     def done(s):
         r = at_rows(s)
@@ -401,6 +393,12 @@
     @pl.when(is_mid)
     def _():
         def stage(it, _):
+            @pl.when(it < STRIPS // 2)
+            def _():
+                for s in range(2):
+                    send_end(2 * it + s).wait_recv()
+                    send_far(2 * it + s).start()
+
             @pl.when(it < STRIPS)
             def _():
                 compute(it)
@@ -473,7 +471,8 @@
             collective_id=0, has_side_effects=True, vmem_limit_bytes=60 * 1024 * 1024),
     )(scalar_field, bin_index, sample_counts, view_order, light_dir, tf_color, tf_opacity)
     if exchange:
-        return result
+        channel = lax.broadcasted_iota(jnp.int32, result.shape, 0)
+        return jnp.where(channel == 3, 1.0 - result, result)
     return composite(lax.all_gather(result[None], "depth", axis=0, tiled=True), view_order)
 
 

time: 50.2 us -> 48.8 us (0.972)
  other arithmetic: 0 us -> 2.4 us
  local copies, waits for them, and re-layouts: 2.29 us -> 0 us
  Pallas kernels: 47.1 us -> 45.6 us
    select_n x0 -> x1, other arithmetic: none -> 2.39 us  [on_device(): return jnp.where(channel == 3, 1.0 - result, result)]
    unnamed x1 -> x0, local copies, waits for them, and re-layouts: 2.29 us -> none
    pallas_call x1, Pallas kernels: 47.1 us -> 45.6 us  [on_device(): pl.pallas_call(functools.partial(kernel, n_depth, n_lat, exchange), out_s...]
where the time goes in v3:
time: 48.8 us; the launch traced here: 48.6 us
  Pallas kernels  45.6 us (93%)
  other arithmetic  2.4 us (5%)
  between operations  0.67 us (1%)
    pallas_call x1, Pallas kernels, on_device(): pl.pallas_call(functools.partial(kernel, n_depth, n_lat, exchange), out_s...  45.6 us
    select_n x1, other arithmetic, on_device(): return jnp.where(channel == 3, 1.0 - result, result)  2.39 us

profile of v3, /device:TPU:0, one launch (start us, length us, event | category | flops | bytes accessed | tf_op | source)
XLA Modules:
  0.0 48.6 jit_solution(8054170094956176307)
XLA Ops:
  0.7 45.6 %shard_map.73 = f32[4,256,256]{2,1,0:T(8,128)} custom-call(f32[1,18,256,256]{3,2,1,0:T(8,128)} %field.1, s32[1,16,256,256]{3,2,1,0:T(8,128)} %bins.1, s32[1,1,1]{2,1,0:T(1,128)S(6)} %copy.8.counts_in, s32[4]{0:T(128)} %order_in.1, f32[3]{0:T(128)} %light_in.1, f32[3,32]{1,0:T(4,128)} %color_in.1, f32[32]{0:T(128)} %opacity_in.1), custom_call_target="tpu_custom_call" | custom-call | tf_op jit(solution)/shard_map/pallas_call | solution.py:443
  46.2 2.4 %subtract_select_fusion = f32[4,256,256]{2,1,0:T(8,128)} fusion(f32[4,256,256]{2,1,0:T(8,128)} %shard_map.73, pred[4]{0:T(512)(128)(4,1)S(1)} %iota_compare_fusion), kind=kLoop, calls=%fused_computation | loop fusion | flops 524288 | bytes 2097156 | tf_op jit(solution)/shard_map/jit(_where)/select_n | solution.py:475
  (1 shorter events, 0.0 us)
